TPU v7x, 32 devices: a whole 2x2x4 slice. The times are simulated.
32 devices in a mesh: band: 8 (over y, x, core), grp: 4 (over z).
Axes of the slice: x: 2, y: 2, z: 4, core: 2. Of those that a mesh axis runs over, the one named last changes fastest.
Arguments:
- spectral: bfloat16 [640, 2, 4, 16, 640], P(('band', 'grp')), may hold values from -6 to 6
- legendre: bfloat16 [640, 640, 640], P(('band', 'grp')), may hold values from -4 to 4
- owner_table: int32 [640], replicated, may hold values from 0 to 639, as said below
Outputs:
- spectral_out: float32 [640, 2, 4, 16, 640], P(('band', 'grp'))
Inputs may be any that keep to these rules, and one draw needn't show every extreme that they name: `owner_table`: A permutation of the zonal wavenumbers. Slot s of the whole array belongs to device s // 20 along band+grp. For each q below 10, slots 2q and 2q + 1 of every device hold wavenumbers whose sum is (4q + 2) * 32 - 1.
All inputs are finite; a program needn't handle non-finite values.
Results may differ from a plain program's by a relative error of at most 0.0067.
Values may be sent and summed in bfloat16 or wider, within the bound.
No kernel may reach another device: no remote copies, remote signals or barrier semaphores. Data moves between devices by JAX's collectives and lax.ppermute only.
A program may use at most 192 MiB of HBM per device.

v0:
```python
import math

import jax
import jax.numpy as jnp
from jax import lax
from jax.sharding import PartitionSpec as P

M = 640
NLAT = 1280
NLON = 2560
FIELDS = 4


def make_trig(wavenumber):
    lon_index = jnp.arange(NLON, dtype=jnp.int32)
    phases = wavenumber[:, None] * lon_index[None, :] % NLON
    angles = phases.astype(jnp.float32) * (2.0 * math.pi / NLON)
    return jnp.stack([jnp.cos(angles), -jnp.sin(angles)], axis=1).astype(jnp.bfloat16)


def on_device(spectral, legendre, owner_table):
    slot_count = spectral.shape[0]
    degrees = spectral.shape[-1]
    levels = spectral.shape[3]
    half_lat = legendre.shape[2]
    band_count = lax.axis_size("band")
    group_count = lax.axis_size("grp")
    device_count = band_count * group_count
    level_block = levels // band_count
    lat_block = NLAT // group_count
    row_total = 2 * FIELDS * levels
    row_width = FIELDS * level_block * lat_block
    slot_start = lax.axis_index(("band", "grp")) * slot_count
    wavenumber = lax.dynamic_slice_in_dim(owner_table, slot_start, slot_count)
    degree_index = jnp.arange(degrees, dtype=jnp.int32)
    keep_mask = (degree_index[None, :] >= wavenumber[:, None]).astype(jnp.bfloat16)
    odd_part = (degree_index[None, :] - wavenumber[:, None]) % 2
    flip_sign = (1 - 2 * odd_part).astype(jnp.bfloat16)
    spec_rows = spectral.reshape(slot_count, row_total, degrees) * keep_mask[:, None, :]
    both_rows = jnp.concatenate([spec_rows, spec_rows * flip_sign[:, None, :]], axis=1)
    halves = jnp.einsum("srn,snt->srt", both_rows, legendre, preferred_element_type=jnp.float32)
    northern = halves[:, :row_total]
    mirrored = halves[:, row_total:]
    fourier = jnp.concatenate([northern, jnp.flip(mirrored, axis=2)], axis=2)
    fourier = fourier.reshape(
        slot_count, 2, FIELDS, band_count, level_block, group_count, lat_block
    )
    fourier = jnp.transpose(fourier, (0, 1, 2, 3, 5, 4, 6))
    fourier_low = (fourier * (1.0 / math.sqrt(degrees))).astype(jnp.bfloat16)
    packed = fourier_low.reshape(1, slot_count, 2, FIELDS, device_count, level_block, lat_block)
    arrived = lax.all_to_all(packed, ("band", "grp"), split_axis=4, concat_axis=0, tiled=True)
    arrived = arrived.reshape(-1, 2, row_width)
    trig_rows = make_trig(owner_table)
    grid_values = jnp.einsum("scw,scl->wl", arrived, trig_rows, preferred_element_type=jnp.float32)
    grid_values = (grid_values * (1.0 / math.sqrt(M))).reshape(
        FIELDS, level_block * lat_block, NLON
    )
    product = (grid_values * jnp.roll(grid_values, -1, axis=0)).astype(jnp.bfloat16)
    zonal_coeffs = jnp.einsum(
        "wl,scl->scw",
        product.reshape(row_width, NLON),
        trig_rows,
        preferred_element_type=jnp.float32,
    )
    zonal_coeffs = (zonal_coeffs * (2.0 / math.sqrt(NLON))).astype(jnp.bfloat16)
    sendback = zonal_coeffs.reshape(device_count, slot_count, 2, FIELDS, 1, level_block, lat_block)
    returned = lax.all_to_all(sendback, ("band", "grp"), split_axis=0, concat_axis=4, tiled=True)
    returned = returned.reshape(
        slot_count, 2, FIELDS, band_count, group_count, level_block, lat_block
    )
    returned = jnp.transpose(returned, (0, 1, 2, 3, 5, 4, 6)).reshape(slot_count, row_total, NLAT)
    northern_part = returned[:, :, :half_lat].astype(jnp.float32)
    mirror_part = jnp.flip(returned[:, :, half_lat:], axis=2).astype(jnp.float32)
    plus_part = (northern_part + mirror_part).astype(jnp.bfloat16)
    minus_part = (northern_part - mirror_part).astype(jnp.bfloat16)
    stacked = jnp.concatenate([plus_part, minus_part], axis=1)
    projected = jnp.einsum("srt,snt->srn", stacked, legendre, preferred_element_type=jnp.float32)
    even_rows = flip_sign[:, None, :] > 0
    chosen = jnp.where(even_rows, projected[:, :row_total], projected[:, row_total:])
    chosen = chosen * keep_mask.astype(jnp.float32)[:, None, :] * (1.0 / math.sqrt(NLAT))
    return chosen.reshape(slot_count, 2, FIELDS, levels, degrees)


def solution(mesh):
    placed = (P(("band", "grp"), None, None, None, None), P(("band", "grp"), None, None), P())
    return jax.shard_map(
        on_device,
        mesh=mesh,
        in_specs=placed,
        out_specs=P(("band", "grp"), None, None, None, None),
        check_vma=False,
    )
```

profile of v0, /device:TPU:0, one launch (start us, length us, event | category | flops | bytes accessed | tf_op | source)
XLA Modules:
  0.0 714.7 jit_solution(15013739568688168741)
XLA Ops:
  5.9 16.1 %fusion.12 = f32[20,256,640]{2,1,0:T(8,128)} fusion(bf16[20,640,640]{2,1,0:T(8,128)(2,1)} %param.4, bf16[20,128,640]{2,1,0:T(8,128)(2,1)S(1)} %get-tuple-element.5, bf16[20,128,640]{2,1,0:T(8,128)(2,1)} %get-tuple-element.6), kind=kOutput, calls=%fused_computation.22 | convolution fusion | flops 4207411200 | bytes 36044800 | tf_op jit(solution)/shard_map/srn,snt->srt/dot_general | solution.py:41
  21.9 11.1 %fusion.37 = (f32[20,128,640]{2,1,0:T(8,128)}, f32[20,128,640]{2,1,0:T(8,128)}) fusion(f32[20,256,640]{2,1,0:T(8,128)} %fusion.12), kind=kLoop, calls=%fused_computation.57 | loop fusion | bytes 26214400 | tf_op jit(solution)/shard_map/slice | solution.py:42
  33.0 53.1 %rev.8 = f32[20,128,640]{2,1,0:T(8,128)} reverse(f32[20,128,640]{2,1,0:T(8,128)} %get-tuple-element.8), dimensions={2} | reverse | bytes 13107200 | tf_op jit(solution)/shard_map/jit(_flip)/rev | solution.py:44
  86.2 7.8 %fusion.1 = bf16[20,128,1280]{2,1,0:T(8,128)(2,1)} fusion(f32[20,128,640]{2,1,0:T(8,128)} %rev.8, f32[20,128,640]{2,1,0:T(8,128)} %get-tuple-element.7), kind=kLoop, calls=%fused_computation.5 | loop fusion | flops 9830400 | bytes 19660800 | tf_op jit(solution)/shard_map/convert_element_type | solution.py:49
  94.0 15.9 %convert_element_type.74 = bf16[20,2,4,8,2,4,320]{6,5,4,3,2,1,0:T(4,128)(2,1)} reshape(bf16[20,128,1280]{2,1,0:T(8,128)(2,1)} %fusion.1) | data formatting | bytes 13107200 | tf_op jit(solution)/shard_map/convert_element_type | solution.py:49
  109.8 12.5 %copy.16 = bf16[20,2,4,8,2,4,320]{6,4,2,1,0,5,3:T(2,128)(2,1)} copy(bf16[20,2,4,8,2,4,320]{6,5,4,3,2,1,0:T(4,128)(2,1)} %convert_element_type.74) | data formatting | bytes 13107200 | tf_op jit(solution)/shard_map/reshape | solution.py:50
  122.3 7.6 %all-to-all-start = ((bf16[1,20,2,4,32,2,320]{6,5,3,2,1,0,4:T(2,128)(2,1)}), bf16[1,20,2,4,32,2,320]{6,5,3,2,1,0,4:T(2,128)(2,1)}, u32[]{:S(2)}, u32[]{:S(2)}) async-start(bf16[1,20,2,4,32,2,320]{6,5,3,2,1,0,4:T(2,128)(2,1)} %bitcast.40), calls=%async_computation | async-start | bytes 15728640 | tf_op jit(solution)/shard_map/all_to_all | solution.py:51
  129.9 29.0 %cosine_convert_fusion = (bf16[640,1,2560]{2,0,1:T(8,128)(2,1)S(1)}, bf16[640,1,2560]{2,0,1:T(8,128)(2,1)}) fusion(s32[640]{0:T(1024)S(1)} %copy-done.2), kind=kLoop, calls=%fused_computation.32 | loop fusion | flops 19660800 | bytes 6556160 | tf_op jit(solution)/shard_map/convert
  159.0 141.4 %all-to-all-done = bf16[1,20,2,4,32,2,320]{6,5,3,2,1,0,4:T(2,128)(2,1)} async-done(((bf16[1,20,2,4,32,2,320]{6,5,3,2,1,0,4:T(2,128)(2,1)}), bf16[1,20,2,4,32,2,320]{6,5,3,2,1,0,4:T(2,128)(2,1)}, u32[]{:S(2)}, u32[]{:S(2)}) %all-to-all-start) | async-done | bytes 6553632 | tf_op jit(solution)/shard_map/all_to_all | solution.py:51
  300.4 22.4 %reshape.196 = bf16[640,2,2560]{2,1,0:T(2,128)(2,1)} reshape(bf16[32,1,20,2,4,1,2,320]{7,6,4,3,2,0,5,1:T(2,128)(2,1)} %bitcast.5) | data formatting | bytes 13107200 | tf_op jit(solution)/shard_map/reshape | solution.py:52
  322.8 23.5 %bitcast_multiply_fusion.1 = f32[2560,2560]{1,0:T(8,128)} fusion(bf16[640,2,2560]{2,1,0:T(2,128)(2,1)} %reshape.196, bf16[640,1,2560]{2,0,1:T(8,128)(2,1)} %get-tuple-element.12, bf16[640,1,2560]{2,0,1:T(8,128)(2,1)S(1)} %get-tuple-element.11), kind=kOutput, calls=%fused_computation.3 | convolution fusion | flops 16787046400 | bytes 39321600 | tf_op jit(solution)/shard_map/scw,scl->wl/dot_general | solution.py:54
  349.7 6.6 slice-done
  356.2 9.0 %pad_maximum_fusion = f32[4,640,2560]{2,1,0:T(8,128)} fusion(f32[1,640,2560]{2,1,0:T(8,128)S(1)} %slice_bitcast_fusion, f32[3,640,2560]{2,1,0:T(8,128)S(1)} %bitcast.38), kind=kLoop, calls=%fused_computation | loop fusion | flops 6553600 | bytes 52428800 | tf_op jit(solution)/shard_map/jit(_roll_static)/concatenate | solution.py:58
  365.2 21.9 %fusion = bf16[2560,2560]{1,0:T(8,128)(2,1)} fusion(f32[2560,2560]{1,0:T(8,128)} %bitcast_multiply_fusion.1, f32[4,640,2560]{2,1,0:T(8,128)} %pad_maximum_fusion), kind=kLoop, calls=%fused_computation.2 | loop fusion | flops 13107200 | bytes 65536000 | tf_op jit(solution)/shard_map/convert_element_type | solution.py:58
  387.1 23.2 %multiply_convert_fusion = bf16[640,2,2560]{2,0,1:T(8,128)(2,1)} fusion(bf16[2560,2560]{1,0:T(8,128)(2,1)} %fusion, bf16[640,1,2560]{2,0,1:T(8,128)(2,1)} %get-tuple-element.12, bf16[640,1,2560]{2,0,1:T(8,128)(2,1)S(1)} %get-tuple-element.11), kind=kOutput, calls=%fused_computation.8 | convolution fusion | flops 16787046400 | bytes 26214400 | tf_op jit(solution)/shard_map/wl,scl->scw/dot_general | solution.py:59
  410.3 18.5 %reshape.190 = bf16[32,20,2,4,1,2,320]{6,5,3,1,0,2,4:T(2,128)(2,1)} reshape(bf16[640,2,2560]{2,0,1:T(8,128)(2,1)} %multiply_convert_fusion) | data formatting | bytes 13107200 | tf_op jit(solution)/shard_map/reshape | solution.py:66
  428.7 9.7 %copy.13 = bf16[32,20,2,4,1,2,320]{6,5,3,1,2,4,0:T(2,128)(2,1)S(1)} copy(bf16[32,20,2,4,1,2,320]{6,5,3,1,0,2,4:T(2,128)(2,1)} %reshape.190) | data formatting | bytes 13107200 | tf_op jit(solution)/shard_map/reshape | solution.py:66
  438.4 179.9 %all_to_all.30 = bf16[32,20,2,4,1,2,320]{6,5,3,1,2,4,0:T(2,128)(2,1)} all-to-all(bf16[32,20,2,4,1,2,320]{6,5,3,1,2,4,0:T(2,128)(2,1)S(1)} %copy.13), channel_id=1, replica_groups=mesh['band'=8,'grp'=4] {'band','grp'}, dimensions={0} | all-to-all | bytes 13107200 | tf_op jit(solution)/shard_map/all_to_all | solution.py:67
  618.3 16.5 %copy.23 = bf16[20,2,4,8,4,2,320]{6,4,5,3,2,1,0:T(4,128)(2,1)} copy(bf16[20,2,4,8,4,2,320]{6,5,2,0,1,4,3:T(2,128)(2,1)} %bitcast.41) | data formatting | bytes 13107200 | tf_op jit(solution)/shard_map/reshape | solution.py:68
  634.8 13.6 %reshape.192 = bf16[20,128,1280]{2,1,0:T(8,128)(2,1)} reshape(bf16[20,2,4,8,2,4,320]{6,5,4,3,2,1,0:T(4,128)(2,1)} %bitcast.39) | data formatting | bytes 13107200 | tf_op jit(solution)/shard_map/reshape | solution.py:71
  650.2 35.3 %rev.9 = bf16[20,128,640]{2,1,0:T(8,128)(2,1)} reverse(bf16[20,128,640]{2,1,0:T(8,128)(2,1)S(1)} %slice-done.1), dimensions={2} | reverse | bytes 6553600 | tf_op jit(solution)/shard_map/jit(_flip)/rev | solution.py:73
  685.6 6.3 fusion.6
  691.8 13.2 %fusion.16 = f32[20,256,640]{2,1,0:T(8,128)} fusion(bf16[20,640,640]{2,1,0:T(8,128)(2,1)} %param.4, bf16[20,128,640]{2,1,0:T(8,128)(2,1)} %get-tuple-element.10, bf16[20,128,640]{2,1,0:T(8,128)(2,1)S(1)} %get-tuple-element.9), kind=kOutput, calls=%fused_computation.26 | convolution fusion | flops 4207411200 | bytes 36044800 | tf_op jit(solution)/shard_map/srt,snt->srn/dot_general | solution.py:77
  705.0 9.1 %fusion.11 = f32[20,128,640]{2,1,0:T(8,128)} fusion(f32[20,256,640]{2,1,0:T(8,128)} %fusion.16, f32[20,640]{1,0:T(8,128)S(1)} %copy-done, pred[20,640]{1,0:T(8,128)(4,1)S(1)} %copy-done.1), kind=kLoop, calls=%fused_computation.19 | loop fusion | flops 4915200 | bytes 19724800 | tf_op jit(solution)/shard_map/mul | solution.py:80
  (14 shorter events, 11.1 us)
Async XLA Ops:
  122.3 7.6 %copy-start.2 = (s32[640]{0:T(1024)S(1)}, s32[640]{0:T(1024)}, u32[]{:S(2)}) copy-start(s32[640]{0:T(1024)} %param.5) | copy-start | bytes 7684
  122.3 178.1 %all-to-all-start = ((bf16[1,20,2,4,32,2,320]{6,5,3,2,1,0,4:T(2,128)(2,1)}), bf16[1,20,2,4,32,2,320]{6,5,3,2,1,0,4:T(2,128)(2,1)}, u32[]{:S(2)}, u32[]{:S(2)}) async-start(bf16[1,20,2,4,32,2,320]{6,5,3,2,1,0,4:T(2,128)(2,1)} %bitcast.40), calls=%async_computation | async-start | bytes 15728640 | tf_op jit(solution)/shard_map/all_to_all | solution.py:51
  349.6 6.6 slice-start
  648.3 1.9 slice-start.1
  691.8 13.2 %copy-start = (f32[20,640]{1,0:T(8,128)S(1)}, f32[20,640]{1,0:T(8,128)}, u32[]{:S(2)}) copy-start(f32[20,640]{1,0:T(8,128)} %get-tuple-element.14) | copy-start | bytes 153604
  691.8 13.2 %copy-start.1 = (pred[20,640]{1,0:T(8,128)(4,1)S(1)}, pred[20,640]{1,0:T(8,128)(4,1)}, u32[]{:S(2)}) copy-start(pred[20,640]{1,0:T(8,128)(4,1)} %get-tuple-element.13) | copy-start | bytes 38404
where the time goes:
time: 726 us; the launch traced here: 715 us
  local copies, waits for them, and re-layouts  221 us (30%)
  blocking collectives  180 us (25%)
  waiting for transfers between devices  141 us (19%)
  other arithmetic  88.2 us (12%)
  matrix products  75.9 us (10%)
  starting transfers between devices  7.59 us (1%)
    all_to_all x1, blocking collectives, on_device(): lax.all_to_all(sendback, ('band', 'grp'), split_axis=0, concat_axis=4, ti...  180 us
    all_to_all x1, waiting for transfers between devices, on_device(): lax.all_to_all(packed, ('band', 'grp'), split_axis=4, concat_axis=0, tile...  141 us
    rev x1, local copies, waits for them, and re-layouts, on_device(): fourier = jnp.concatenate([northern, jnp.flip(mirrored, axis=2)], axis=2)  53.1 us
    rev x1, local copies, waits for them, and re-layouts, on_device(): jnp.flip(returned[:, :, half_lat:], axis=2).astype(jnp.float32)  35.3 us
    another operation x1, other arithmetic  29 us
    reshape x2, local copies, waits for them, and re-layouts, on_device(): zonal_coeffs.reshape(device_count, slot_count, 2, FIELDS, 1, level_block,...  28.2 us
    dot_general x1, matrix products, on_device(): jnp.einsum('scw,scl->wl', arrived, trig_rows, preferred_element_type=jnp....  23.5 us
    dot_general x1, matrix products, on_device(): jnp.einsum('wl,scl->scw', product.reshape(row_width, NLON), trig_rows, pr...  23.2 us
  transfers between devices with their start and end apart: 1, of which 1 were waited for; matrix products, arithmetic and copies ran while one was open for 4% of the time, Pallas kernels for 0%

commit v1 on v0

v1 whole, which is shorter than its diff:
```python
import functools
import math

import jax
import jax.numpy as jnp
from jax import lax
from jax.experimental import pallas as pl
from jax.experimental.pallas import tpu as pltpu
from jax.sharding import PartitionSpec as P

LANES = 128
AXES = ("band", "grp")
VMEM_BYTES = 56 * 1024 * 1024


def synthesis_kernel(slots, levels, fields, scale, spec_ref, keep_ref, flip_ref, table_ref, out_ref, rows_ref):
    step = pl.program_id(0)
    block = spec_ref.shape[0]
    row_total = spec_ref.shape[1]
    stride = 2 * slots
    for j in range(block):
        kept = spec_ref[j] * keep_ref[j]
        both = jnp.concatenate([kept, spec_ref[j] * flip_ref[j]], axis=0)
        halves = jnp.dot(both, table_ref[j], preferred_element_type=jnp.float32) * scale
        first = 2 * (step * block + j)
        for hemi in range(2):
            for part in range(2):
                for field in range(fields):
                    at = hemi * row_total + (part * fields + field) * levels
                    target = hemi * levels * stride + first + part
                    rows_ref[field, pl.ds(target, levels, stride=stride), :] = halves[at : at + levels]

    @pl.when(step == pl.num_programs(0) - 1)
    def _():
        for field in range(fields):
            out_ref[:, pl.ds(field * LANES, LANES)] = rows_ref[field].astype(out_ref.dtype)


def synthesize(spec_rows, keep, flip, legendre, tile, fields, levels):
    slots, row_total, degrees = spec_rows.shape
    block = 4
    rows = 2 * levels * 2 * slots
    return pl.pallas_call(
        functools.partial(synthesis_kernel, slots, levels, fields, 1.0 / math.sqrt(degrees)),
        grid=(slots // block,),
        in_specs=[
            pl.BlockSpec((block, row_total, degrees), lambda i: (i, 0, 0)),
            pl.BlockSpec((block, 1, degrees), lambda i: (i, 0, 0)),
            pl.BlockSpec((block, 1, degrees), lambda i: (i, 0, 0)),
            pl.BlockSpec((block, degrees, LANES), lambda i: (i, 0, tile)),
        ],
        out_specs=pl.BlockSpec((rows, fields * LANES), lambda i: (0, 0)),
        out_shape=jax.ShapeDtypeStruct((rows, fields * LANES), jnp.bfloat16),
        scratch_shapes=[pltpu.VMEM((fields, rows, LANES), jnp.float32)],
        compiler_params=pltpu.CompilerParams(vmem_limit_bytes=VMEM_BYTES),
        cost_estimate=pl.CostEstimate(
            flops=4 * slots * row_total * degrees * LANES,
            bytes_accessed=2 * slots * degrees * (row_total + LANES) + 2 * rows * fields * LANES,
            transcendentals=0,
        ),
        name="synthesis",
    )(spec_rows, keep, flip, legendre)


def longitude_kernel(grid_scale, zonal_scale, rows_ref, by_lon_ref, by_wave_ref, out_ref, sum_ref):
    step = pl.program_id(0)
    values = jnp.dot(by_lon_ref[...], rows_ref[...], preferred_element_type=jnp.float32) * grid_scale
    following = jnp.concatenate([values[:, LANES:], values[:, :LANES]], axis=1)
    product = (values * following).astype(jnp.bfloat16)
    share = jnp.dot(by_wave_ref[...], product, preferred_element_type=jnp.float32)

    @pl.when(step == 0)
    def _():
        sum_ref[...] = share

    @pl.when(step > 0)
    def _():
        sum_ref[...] += share

    @pl.when(step == pl.num_programs(0) - 1)
    def _():
        out_ref[...] = (sum_ref[...] * zonal_scale).astype(out_ref.dtype)


def longitudes(rows, by_lon, by_wave):
    depth, width = rows.shape
    lon_count = by_lon.shape[0]
    lon_block = lon_count // 5
    return pl.pallas_call(
        functools.partial(longitude_kernel, 1.0 / math.sqrt(depth // 2), 2.0 / math.sqrt(lon_count)),
        grid=(lon_count // lon_block,),
        in_specs=[
            pl.BlockSpec((depth, width), lambda i: (0, 0)),
            pl.BlockSpec((lon_block, depth), lambda i: (i, 0)),
            pl.BlockSpec((depth, lon_block), lambda i: (0, i)),
        ],
        out_specs=pl.BlockSpec((depth, width), lambda i: (0, 0)),
        out_shape=jax.ShapeDtypeStruct((depth, width), jnp.bfloat16),
        scratch_shapes=[pltpu.VMEM((depth, width), jnp.float32)],
        compiler_params=pltpu.CompilerParams(vmem_limit_bytes=VMEM_BYTES),
        cost_estimate=pl.CostEstimate(
            flops=4 * depth * width * lon_count,
            bytes_accessed=4 * depth * (width + lon_count),
            transcendentals=0,
        ),
        name="longitudes",
    )(rows, by_lon, by_wave)


def fold_kernel(slots, levels, fields, rows_ref, out_ref, plus_ref, minus_ref):
    half = rows_ref.shape[0] // 2
    stride = 2 * slots
    for field in range(fields):
        lanes = pl.ds(field * LANES, LANES)
        north = rows_ref[:half, lanes].astype(jnp.float32)
        south = rows_ref[half:, lanes].astype(jnp.float32)
        plus_ref[field] = north + south
        minus_ref[field] = north - south
    for slot in range(slots):
        for which, folded_ref in enumerate((plus_ref, minus_ref)):
            for part in range(2):
                for field in range(fields):
                    at = ((which * 2 + part) * fields + field) * levels
                    out_ref[slot, at : at + levels, :] = folded_ref[
                        field, pl.ds(2 * slot + part, levels, stride=stride), :
                    ].astype(out_ref.dtype)


def fold(rows, slots, levels, fields):
    row_total = 2 * fields * levels
    shape = (slots, 2 * row_total, LANES)
    half = pltpu.VMEM((fields, rows.shape[0] // 2, LANES), jnp.float32)
    return pl.pallas_call(
        functools.partial(fold_kernel, slots, levels, fields),
        in_specs=[pl.BlockSpec(rows.shape, lambda: (0, 0))],
        out_specs=pl.BlockSpec(shape, lambda: (0, 0, 0)),
        out_shape=jax.ShapeDtypeStruct(shape, jnp.bfloat16),
        scratch_shapes=[half, half],
        compiler_params=pltpu.CompilerParams(vmem_limit_bytes=VMEM_BYTES),
        cost_estimate=pl.CostEstimate(flops=2 * rows.size, bytes_accessed=4 * rows.size, transcendentals=0),
        name="fold",
    )(rows)


def analysis_kernel(tiles, *refs):
    folded_refs = refs[:tiles]
    even_ref, odd_ref, table_ref, out_ref = refs[tiles:]
    row_total = out_ref.shape[1]
    for j in range(out_ref.shape[0]):
        folded = jnp.concatenate([ref[j] for ref in folded_refs], axis=1)
        sums = lax.dot_general(
            folded, table_ref[j], (((1,), (1,)), ((), ())), preferred_element_type=jnp.float32
        )
        out_ref[j] = sums[:row_total] * even_ref[j] + sums[row_total:] * odd_ref[j]


def analyze(folded, even, odd, legendre, row_total):
    slots, degrees, lat_count = legendre.shape
    block = 2
    tiles = len(folded)
    folded_spec = pl.BlockSpec((block, 2 * row_total, LANES), lambda i: (i, 0, 0))
    mask_spec = pl.BlockSpec((block, 1, degrees), lambda i: (i, 0, 0))
    return pl.pallas_call(
        functools.partial(analysis_kernel, tiles),
        grid=(slots // block,),
        in_specs=[folded_spec] * tiles
        + [mask_spec, mask_spec, pl.BlockSpec((block, degrees, lat_count), lambda i: (i, 0, 0))],
        out_specs=pl.BlockSpec((block, row_total, degrees), lambda i: (i, 0, 0)),
        out_shape=jax.ShapeDtypeStruct((slots, row_total, degrees), jnp.float32),
        compiler_params=pltpu.CompilerParams(vmem_limit_bytes=VMEM_BYTES),
        cost_estimate=pl.CostEstimate(
            flops=4 * slots * row_total * degrees * lat_count,
            bytes_accessed=2 * slots * (degrees * lat_count + 2 * row_total * (lat_count + degrees)),
            transcendentals=0,
        ),
        name="analysis",
    )(*folded, even, odd, legendre)


def trig_tables(owner_table, lon_count):
    waves = jnp.repeat(owner_table, 2)
    quarter = jnp.tile(jnp.array([0, lon_count // 4], jnp.int32), owner_table.shape[0])
    lon_index = jnp.arange(lon_count, dtype=jnp.int32)

    def table(wave, turn, lon):
        phase = (wave * lon + turn) % lon_count
        return jnp.cos(phase.astype(jnp.float32) * (2.0 * math.pi / lon_count)).astype(jnp.bfloat16)

    by_lon = table(waves[None, :], quarter[None, :], lon_index[:, None])
    by_wave = table(waves[:, None], quarter[:, None], lon_index[None, :])
    return by_lon, by_wave


def exchange(rows):
    return lax.all_to_all(rows, AXES, split_axis=0, concat_axis=0, tiled=True)


def by_hemisphere_and_level(spectral, legendre, owner_table):
    slots, _, fields, levels, degrees = spectral.shape
    half_lat = legendre.shape[2]
    lon_count = 4 * half_lat
    row_total = 2 * fields * levels
    tiles = half_lat // LANES
    wavenumber = lax.dynamic_slice_in_dim(owner_table, lax.axis_index(AXES) * slots, slots)
    distance = jnp.arange(degrees, dtype=jnp.int32)[None, :] - wavenumber[:, None]
    kept = distance >= 0
    is_odd = distance % 2 != 0
    keep = kept.astype(jnp.bfloat16)[:, None, :]
    flip = jnp.where(is_odd, -keep[:, 0], keep[:, 0])[:, None, :]
    scale = 1.0 / math.sqrt(2 * half_lat)
    even = jnp.where(kept & ~is_odd, scale, 0.0).astype(jnp.float32)[:, None, :]
    odd = jnp.where(kept & is_odd, scale, 0.0).astype(jnp.float32)[:, None, :]
    spec_rows = spectral.reshape(slots, row_total, degrees)
    sent = [synthesize(spec_rows, keep, flip, legendre, t, fields, levels) for t in range(tiles)]
    arrived = [exchange(rows) for rows in sent]
    by_lon, by_wave = trig_tables(owner_table, lon_count)
    zonal = [longitudes(rows, by_lon, by_wave) for rows in arrived]
    returned = [exchange(rows) for rows in zonal]
    folded = [fold(rows, slots, levels, fields) for rows in returned]
    out = analyze(folded, even, odd, legendre, row_total)
    return out.reshape(slots, 2, fields, levels, degrees)


def make_trig(wavenumber, lon_count):
    lon_index = jnp.arange(lon_count, dtype=jnp.int32)
    phases = wavenumber[:, None] * lon_index[None, :] % lon_count
    angles = phases.astype(jnp.float32) * (2.0 * math.pi / lon_count)
    return jnp.stack([jnp.cos(angles), -jnp.sin(angles)], axis=1).astype(jnp.bfloat16)


def by_level_and_latitude(spectral, legendre, owner_table):
    slot_count, _, fields, levels, degrees = spectral.shape
    half_lat = legendre.shape[2]
    lat_count = 2 * half_lat
    lon_count = 2 * lat_count
    wave_count = owner_table.shape[0]
    band_count = lax.axis_size("band")
    group_count = lax.axis_size("grp")
    device_count = band_count * group_count
    level_block = levels // band_count
    lat_block = lat_count // group_count
    row_total = 2 * fields * levels
    row_width = fields * level_block * lat_block
    slot_start = lax.axis_index(("band", "grp")) * slot_count
    wavenumber = lax.dynamic_slice_in_dim(owner_table, slot_start, slot_count)
    degree_index = jnp.arange(degrees, dtype=jnp.int32)
    keep_mask = (degree_index[None, :] >= wavenumber[:, None]).astype(jnp.bfloat16)
    odd_part = (degree_index[None, :] - wavenumber[:, None]) % 2
    flip_sign = (1 - 2 * odd_part).astype(jnp.bfloat16)
    spec_rows = spectral.reshape(slot_count, row_total, degrees) * keep_mask[:, None, :]
    both_rows = jnp.concatenate([spec_rows, spec_rows * flip_sign[:, None, :]], axis=1)
    halves = jnp.einsum("srn,snt->srt", both_rows, legendre, preferred_element_type=jnp.float32)
    northern = halves[:, :row_total]
    mirrored = halves[:, row_total:]
    fourier = jnp.concatenate([northern, jnp.flip(mirrored, axis=2)], axis=2)
    fourier = fourier.reshape(
        slot_count, 2, fields, band_count, level_block, group_count, lat_block
    )
    fourier = jnp.transpose(fourier, (0, 1, 2, 3, 5, 4, 6))
    fourier_low = (fourier * (1.0 / math.sqrt(degrees))).astype(jnp.bfloat16)
    packed = fourier_low.reshape(1, slot_count, 2, fields, device_count, level_block, lat_block)
    arrived = lax.all_to_all(packed, ("band", "grp"), split_axis=4, concat_axis=0, tiled=True)
    arrived = arrived.reshape(-1, 2, row_width)
    trig_rows = make_trig(owner_table, lon_count)
    grid_values = jnp.einsum("scw,scl->wl", arrived, trig_rows, preferred_element_type=jnp.float32)
    grid_values = (grid_values * (1.0 / math.sqrt(wave_count))).reshape(
        fields, level_block * lat_block, lon_count
    )
    product = (grid_values * jnp.roll(grid_values, -1, axis=0)).astype(jnp.bfloat16)
    zonal_coeffs = jnp.einsum(
        "wl,scl->scw",
        product.reshape(row_width, lon_count),
        trig_rows,
        preferred_element_type=jnp.float32,
    )
    zonal_coeffs = (zonal_coeffs * (2.0 / math.sqrt(lon_count))).astype(jnp.bfloat16)
    sendback = zonal_coeffs.reshape(device_count, slot_count, 2, fields, 1, level_block, lat_block)
    returned = lax.all_to_all(sendback, ("band", "grp"), split_axis=0, concat_axis=4, tiled=True)
    returned = returned.reshape(
        slot_count, 2, fields, band_count, group_count, level_block, lat_block
    )
    returned = jnp.transpose(returned, (0, 1, 2, 3, 5, 4, 6)).reshape(slot_count, row_total, lat_count)
    northern_part = returned[:, :, :half_lat].astype(jnp.float32)
    mirror_part = jnp.flip(returned[:, :, half_lat:], axis=2).astype(jnp.float32)
    plus_part = (northern_part + mirror_part).astype(jnp.bfloat16)
    minus_part = (northern_part - mirror_part).astype(jnp.bfloat16)
    stacked = jnp.concatenate([plus_part, minus_part], axis=1)
    projected = jnp.einsum("srt,snt->srn", stacked, legendre, preferred_element_type=jnp.float32)
    even_rows = flip_sign[:, None, :] > 0
    chosen = jnp.where(even_rows, projected[:, :row_total], projected[:, row_total:])
    chosen = chosen * keep_mask.astype(jnp.float32)[:, None, :] * (1.0 / math.sqrt(lat_count))
    return chosen.reshape(slot_count, 2, fields, levels, degrees)


def on_device(spectral, legendre, owner_table):
    slots, _, _, levels, _ = spectral.shape
    whole_hemispheres = lax.axis_size("band") * lax.axis_size("grp") == 2 * levels
    if whole_hemispheres and legendre.shape[2] % LANES == 0 and slots % 4 == 0 and levels % 8 == 0:
        return by_hemisphere_and_level(spectral, legendre, owner_table)
    return by_level_and_latitude(spectral, legendre, owner_table)


def solution(mesh):
    placed = (P(("band", "grp"), None, None, None, None), P(("band", "grp"), None, None), P())
    return jax.shard_map(
        on_device,
        mesh=mesh,
        in_specs=placed,
        out_specs=P(("band", "grp"), None, None, None, None),
        check_vma=False,
    )
```

time: 726 us -> 475 us (0.65); the launches traced: 715 us -> 472 us
  local copies, waits for them, and re-layouts: 221 us -> 3.59 us
  blocking collectives: 180 us -> 0 us
  Pallas kernels: 0 us -> 130 us
  matrix products: 75.9 us -> 0 us
  starting transfers between devices: 7.59 us -> 49.7 us
  waiting for transfers between devices: 141 us -> 182 us
  other arithmetic: 88.2 us -> 107 us
    all_to_all x1 -> x0, blocking collectives: 180 us -> none  [on_device(): lax.all_to_all(sendback, ('band', 'grp'), split_axis=0, concat_axis=4, ti...]
    pallas_call x0 -> x16, Pallas kernels: none -> 130 us  [the longest x5 63.2 us: longitudes(): pl.pallas_call(functools.partial(longitude_kernel, 1.0 / math.sqrt(depth...]
    reshape x6 -> x0, local copies, waits for them, and re-layouts: 93.1 us -> none  [the longest x2 28.2 us: on_device(): zonal_coeffs.reshape(device_count, slot_count, 2, FIELDS, 1, level_block,...]
    rev x2 -> x0, local copies, waits for them, and re-layouts: 88.5 us -> none  [the longest x1 53.1 us: on_device(): fourier = jnp.concatenate([northern, jnp.flip(mirrored, axis=2)], axis=2)]
    dot_general x4 -> x0, matrix products: 75.9 us -> none  [the longest x1 23.5 us: on_device(): jnp.einsum('scw,scl->wl', arrived, trig_rows, preferred_element_type=jnp....]
    convert_element_type x4 -> x3, other arithmetic: 36.1 us -> 105 us  [the longest x2 104 us: table(): jnp.cos(phase.astype(jnp.float32) * (2.0 * math.pi / lon_count))]
    all_to_all x1 -> x10, starting transfers between devices: 7.59 us -> 49.7 us  [exchange(): return lax.all_to_all(rows, AXES, split_axis=0, concat_axis=0, tiled=True)]
    all_to_all x1 -> x10, waiting for transfers between devices: 141 us -> 182 us  [exchange(): return lax.all_to_all(rows, AXES, split_axis=0, concat_axis=0, tiled=True)]
  transfers between devices with their start and end apart: 1 -> 10, of which waited for: 1 -> 9; matrix products, arithmetic and copies ran while one was open for 4% -> 22% of each run, Pallas kernels for 0% -> 22%
where the time goes in v1:
time: 475 us; the launch traced here: 472 us
  waiting for transfers between devices  182 us (38%)
  Pallas kernels  130 us (27%)
  other arithmetic  107 us (23%)
  starting transfers between devices  49.7 us (10%)
    all_to_all x10, waiting for transfers between devices, exchange(): return lax.all_to_all(rows, AXES, split_axis=0, concat_axis=0, tiled=True)  182 us
    convert_element_type x2, other arithmetic, table(): jnp.cos(phase.astype(jnp.float32) * (2.0 * math.pi / lon_count))  104 us
    pallas_call x5, Pallas kernels, longitudes(): pl.pallas_call(functools.partial(longitude_kernel, 1.0 / math.sqrt(depth...  63.2 us
    all_to_all x10, starting transfers between devices, exchange(): return lax.all_to_all(rows, AXES, split_axis=0, concat_axis=0, tiled=True)  49.7 us
    pallas_call x5, Pallas kernels, synthesize(): pl.pallas_call(functools.partial(synthesis_kernel, slots, levels, fields,...  34.2 us
    pallas_call x1, Pallas kernels, analyze(): pl.pallas_call(functools.partial(analysis_kernel, tiles), grid=(slots //...  16.5 us
    pallas_call x5, Pallas kernels, fold(): pl.pallas_call(functools.partial(fold_kernel, slots, levels, fields), in_...  16 us
  transfers between devices with their start and end apart: 10, of which 9 were waited for; matrix products, arithmetic and copies ran while one was open for 22% of the time, Pallas kernels for 22%

profile of v1, /device:TPU:0, one launch (start us, length us, event | category | flops | bytes accessed | tf_op | source)
XLA Modules:
  0.0 472.1 jit_solution(6947080887971950640)
XLA Ops:
  2.4 6.8 %synthesis.6 = bf16[1280,512]{1,0:T(8,128)(2,1)} custom-call(bf16[20,128,640]{2,1,0:T(8,128)(2,1)} %bitcast.22, bf16[20,1,640]{2,1,0:T(2,128)(2,1)} %fusion.17.keep_ref, bf16[20,1,640]{2,1,0:T(2,128)(2,1)} %negate_select_fusion.flip_ref, bf16[20,640,640]{2,1,0:T(8,128)(2,1)} %refs_7_.1), custom_call_target="tpu_custom_call" | custom-call | flops 838860800 | bytes 7864320 | tf_op jit(solution)/shard_map/synthesis/pallas_call | solution.py:43
  9.2 7.3 %all-to-all-start.2 = ((bf16[32,40,512]{2,1,0:T(8,128)(2,1)}), bf16[32,40,512]{2,1,0:T(8,128)(2,1)S(1)}, u32[]{:S(2)}, u32[]{:S(2)}) async-start(bf16[32,40,512]{2,1,0:T(8,128)(2,1)} %bitcast.31), calls=%async_computation.2 | async-start | bytes 2621440 | tf_op jit(solution)/shard_map/all_to_all | solution.py:195
  16.5 6.9 %synthesis.7 = bf16[1280,512]{1,0:T(8,128)(2,1)} custom-call(bf16[20,128,640]{2,1,0:T(8,128)(2,1)} %bitcast.23, bf16[20,1,640]{2,1,0:T(2,128)(2,1)} %fusion.17.keep_ref, bf16[20,1,640]{2,1,0:T(2,128)(2,1)} %negate_select_fusion.flip_ref, bf16[20,640,640]{2,1,0:T(8,128)(2,1)} %refs_7_.1), custom_call_target="tpu_custom_call" | custom-call | flops 838860800 | bytes 7864320 | tf_op jit(solution)/shard_map/synthesis/pallas_call | solution.py:43
  23.4 23.6 %all-to-all-done.2 = bf16[32,40,512]{2,1,0:T(8,128)(2,1)S(1)} async-done(((bf16[32,40,512]{2,1,0:T(8,128)(2,1)}), bf16[32,40,512]{2,1,0:T(8,128)(2,1)S(1)}, u32[]{:S(2)}, u32[]{:S(2)}) %all-to-all-start.2) | async-done | bytes 1310752 | tf_op jit(solution)/shard_map/all_to_all | solution.py:195
  51.6 6.8 %synthesis.8 = bf16[1280,512]{1,0:T(8,128)(2,1)} custom-call(bf16[20,128,640]{2,1,0:T(8,128)(2,1)} %bitcast.24, bf16[20,1,640]{2,1,0:T(2,128)(2,1)} %fusion.17.keep_ref, bf16[20,1,640]{2,1,0:T(2,128)(2,1)} %negate_select_fusion.flip_ref, bf16[20,640,640]{2,1,0:T(8,128)(2,1)} %refs_7_.1), custom_call_target="tpu_custom_call" | custom-call | flops 838860800 | bytes 7864320 | tf_op jit(solution)/shard_map/synthesis/pallas_call | solution.py:43
  58.4 23.7 %all-to-all-done.4 = bf16[32,40,512]{2,1,0:T(8,128)(2,1)S(1)} async-done(((bf16[32,40,512]{2,1,0:T(8,128)(2,1)}), bf16[32,40,512]{2,1,0:T(8,128)(2,1)S(1)}, u32[]{:S(2)}, u32[]{:S(2)}) %all-to-all-start.4) | async-done | bytes 1310752 | tf_op jit(solution)/shard_map/all_to_all | solution.py:195
  86.7 6.8 %synthesis.9 = bf16[1280,512]{1,0:T(8,128)(2,1)} custom-call(bf16[20,128,640]{2,1,0:T(8,128)(2,1)} %bitcast.25, bf16[20,1,640]{2,1,0:T(2,128)(2,1)} %fusion.17.keep_ref, bf16[20,1,640]{2,1,0:T(2,128)(2,1)} %negate_select_fusion.flip_ref, bf16[20,640,640]{2,1,0:T(8,128)(2,1)} %refs_7_.1), custom_call_target="tpu_custom_call" | custom-call | flops 838860800 | bytes 7864320 | tf_op jit(solution)/shard_map/synthesis/pallas_call | solution.py:43
  93.5 23.7 %all-to-all-done.6 = bf16[32,40,512]{2,1,0:T(8,128)(2,1)S(1)} async-done(((bf16[32,40,512]{2,1,0:T(8,128)(2,1)}), bf16[32,40,512]{2,1,0:T(8,128)(2,1)S(1)}, u32[]{:S(2)}, u32[]{:S(2)}) %all-to-all-start.6) | async-done | bytes 1310752 | tf_op jit(solution)/shard_map/all_to_all | solution.py:195
  123.5 6.9 %synthesis.5 = bf16[1280,512]{1,0:T(8,128)(2,1)} custom-call(bf16[20,128,640]{2,1,0:T(8,128)(2,1)} %bitcast.26, bf16[20,1,640]{2,1,0:T(2,128)(2,1)} %fusion.17.keep_ref, bf16[20,1,640]{2,1,0:T(2,128)(2,1)} %negate_select_fusion.flip_ref, bf16[20,640,640]{2,1,0:T(8,128)(2,1)} %refs_7_.1), custom_call_target="tpu_custom_call" | custom-call | flops 838860800 | bytes 7864320 | tf_op jit(solution)/shard_map/synthesis/pallas_call | solution.py:43
  130.4 23.0 %all-to-all-done.8 = bf16[32,40,512]{2,1,0:T(8,128)(2,1)S(1)} async-done(((bf16[32,40,512]{2,1,0:T(8,128)(2,1)}), bf16[32,40,512]{2,1,0:T(8,128)(2,1)S(1)}, u32[]{:S(2)}, u32[]{:S(2)}) %all-to-all-start.8) | async-done | bytes 1310752 | tf_op jit(solution)/shard_map/all_to_all | solution.py:195
  158.1 51.4 %fusion.3.by_lon_ref = bf16[2560,1280]{1,0:T(8,128)(2,1)} fusion(s32[1280]{0:T(1024)S(1)} %add.60, s32[1280]{0:T(1024)S(1)} %mul.48), kind=kLoop, calls=%fused_computation.5 | loop fusion | flops 36044800 | bytes 6563840 | tf_op jit(solution)/shard_map/convert_element_type | solution.py:187
  209.4 52.9 %fusion.7.by_wave_ref = bf16[1280,2560]{1,0:T(8,128)(2,1)} fusion(s32[1280]{0:T(1024)S(1)} %add.60, s32[1280]{0:T(1024)S(1)} %mul.48), kind=kLoop, calls=%fused_computation.9 | loop fusion | flops 36044800 | bytes 6563840 | tf_op jit(solution)/shard_map/convert_element_type | solution.py:187
  262.3 12.6 %longitudes.6 = bf16[1280,512]{1,0:T(8,128)(2,1)} custom-call(bf16[1280,512]{1,0:T(8,128)(2,1)} %bitcast.40, bf16[2560,1280]{1,0:T(8,128)(2,1)} %fusion.3.by_lon_ref, bf16[1280,2560]{1,0:T(8,128)(2,1)} %fusion.7.by_wave_ref), custom_call_target="tpu_custom_call" | custom-call | flops 6710886400 | bytes 15728640 | tf_op jit(solution)/shard_map/longitudes/pallas_call | solution.py:89
  274.9 5.7 %all-to-all-start.3 = ((bf16[32,40,512]{2,1,0:T(8,128)(2,1)}), bf16[32,40,512]{2,1,0:T(8,128)(2,1)S(1)}, u32[]{:S(2)}, u32[]{:S(2)}) async-start(bf16[32,40,512]{2,1,0:T(8,128)(2,1)} %bitcast.44), calls=%async_computation.3 | async-start | bytes 2621440 | tf_op jit(solution)/shard_map/all_to_all | solution.py:195
  280.6 12.7 %longitudes.7 = bf16[1280,512]{1,0:T(8,128)(2,1)} custom-call(bf16[1280,512]{1,0:T(8,128)(2,1)} %bitcast.39, bf16[2560,1280]{1,0:T(8,128)(2,1)} %fusion.3.by_lon_ref, bf16[1280,2560]{1,0:T(8,128)(2,1)} %fusion.7.by_wave_ref), custom_call_target="tpu_custom_call" | custom-call | flops 6710886400 | bytes 15728640 | tf_op jit(solution)/shard_map/longitudes/pallas_call | solution.py:89
  293.3 17.8 %all-to-all-done.3 = bf16[32,40,512]{2,1,0:T(8,128)(2,1)S(1)} async-done(((bf16[32,40,512]{2,1,0:T(8,128)(2,1)}), bf16[32,40,512]{2,1,0:T(8,128)(2,1)S(1)}, u32[]{:S(2)}, u32[]{:S(2)}) %all-to-all-start.3) | async-done | bytes 1310752 | tf_op jit(solution)/shard_map/all_to_all | solution.py:195
  315.6 12.7 %longitudes.8 = bf16[1280,512]{1,0:T(8,128)(2,1)} custom-call(bf16[1280,512]{1,0:T(8,128)(2,1)} %bitcast.38, bf16[2560,1280]{1,0:T(8,128)(2,1)} %fusion.3.by_lon_ref, bf16[1280,2560]{1,0:T(8,128)(2,1)} %fusion.7.by_wave_ref), custom_call_target="tpu_custom_call" | custom-call | flops 6710886400 | bytes 15728640 | tf_op jit(solution)/shard_map/longitudes/pallas_call | solution.py:89
  328.3 17.8 %all-to-all-done.5 = bf16[32,40,512]{2,1,0:T(8,128)(2,1)S(1)} async-done(((bf16[32,40,512]{2,1,0:T(8,128)(2,1)}), bf16[32,40,512]{2,1,0:T(8,128)(2,1)S(1)}, u32[]{:S(2)}, u32[]{:S(2)}) %all-to-all-start.5) | async-done | bytes 1310752 | tf_op jit(solution)/shard_map/all_to_all | solution.py:195
  350.9 12.6 %longitudes.9 = bf16[1280,512]{1,0:T(8,128)(2,1)} custom-call(bf16[1280,512]{1,0:T(8,128)(2,1)} %bitcast.37, bf16[2560,1280]{1,0:T(8,128)(2,1)} %fusion.3.by_lon_ref, bf16[1280,2560]{1,0:T(8,128)(2,1)} %fusion.7.by_wave_ref), custom_call_target="tpu_custom_call" | custom-call | flops 6710886400 | bytes 15728640 | tf_op jit(solution)/shard_map/longitudes/pallas_call | solution.py:89
  363.5 17.7 %all-to-all-done.7 = bf16[32,40,512]{2,1,0:T(8,128)(2,1)S(1)} async-done(((bf16[32,40,512]{2,1,0:T(8,128)(2,1)}), bf16[32,40,512]{2,1,0:T(8,128)(2,1)S(1)}, u32[]{:S(2)}, u32[]{:S(2)}) %all-to-all-start.7) | async-done | bytes 1310752 | tf_op jit(solution)/shard_map/all_to_all | solution.py:195
  385.7 12.6 %longitudes.5 = bf16[1280,512]{1,0:T(8,128)(2,1)} custom-call(bf16[1280,512]{1,0:T(8,128)(2,1)} %bitcast.41, bf16[2560,1280]{1,0:T(8,128)(2,1)} %fusion.3.by_lon_ref, bf16[1280,2560]{1,0:T(8,128)(2,1)} %fusion.7.by_wave_ref), custom_call_target="tpu_custom_call" | custom-call | flops 6710886400 | bytes 15728640 | tf_op jit(solution)/shard_map/longitudes/pallas_call | solution.py:89
  398.4 17.9 %all-to-all-done.9 = bf16[32,40,512]{2,1,0:T(8,128)(2,1)S(1)} async-done(((bf16[32,40,512]{2,1,0:T(8,128)(2,1)}), bf16[32,40,512]{2,1,0:T(8,128)(2,1)S(1)}, u32[]{:S(2)}, u32[]{:S(2)}) %all-to-all-start.9) | async-done | bytes 1310752 | tf_op jit(solution)/shard_map/all_to_all | solution.py:195
  434.6 16.7 %all-to-all-done.1 = bf16[32,40,512]{2,1,0:T(8,128)(2,1)S(1)} async-done(((bf16[32,40,512]{2,1,0:T(8,128)(2,1)}), bf16[32,40,512]{2,1,0:T(8,128)(2,1)S(1)}, u32[]{:S(2)}, u32[]{:S(2)}) %all-to-all-start.1) | async-done | bytes 1310752 | tf_op jit(solution)/shard_map/all_to_all | solution.py:195
  455.6 16.5 %analysis.1 = f32[20,128,640]{2,1,0:T(8,128)} custom-call(bf16[20,256,128]{2,1,0:T(8,128)(2,1)} %fold.5.refs_0_, bf16[20,256,128]{2,1,0:T(8,128)(2,1)} %fold.6.refs_1_, bf16[20,256,128]{2,1,0:T(8,128)(2,1)} %fold.7.refs_2_, bf16[20,256,128]{2,1,0:T(8,128)(2,1)} %fold.8.refs_3_, bf16[20,256,128]{2,1,0:T(8,128)(2,1)} %fold.9.refs_4_, ...), custom_call_target="tpu_custom_call" | custom-call | flops 4194304000 | bytes 29491200 | tf_op jit(solution)/shard_map/analysis/pallas_call | solution.py:163
  (45 shorter events, 58.9 us)
Async XLA Ops:
  9.2 37.8 %all-to-all-start.2 = ((bf16[32,40,512]{2,1,0:T(8,128)(2,1)}), bf16[32,40,512]{2,1,0:T(8,128)(2,1)S(1)}, u32[]{:S(2)}, u32[]{:S(2)}) async-start(bf16[32,40,512]{2,1,0:T(8,128)(2,1)} %bitcast.31), calls=%async_computation.2 | async-start | bytes 2621440 | tf_op jit(solution)/shard_map/all_to_all | solution.py:195
  47.0 11.4 %copy-start.8 = (bf16[32,40,512]{2,1,0:T(8,128)(2,1)}, bf16[32,40,512]{2,1,0:T(8,128)(2,1)S(1)}, u32[]{:S(2)}) copy-start(bf16[32,40,512]{2,1,0:T(8,128)(2,1)S(1)} %all-to-all-done.2) | copy-start | bytes 3932164
  47.0 35.0 %all-to-all-start.4 = ((bf16[32,40,512]{2,1,0:T(8,128)(2,1)}), bf16[32,40,512]{2,1,0:T(8,128)(2,1)S(1)}, u32[]{:S(2)}, u32[]{:S(2)}) async-start(bf16[32,40,512]{2,1,0:T(8,128)(2,1)} %bitcast.29), calls=%async_computation.4 | async-start | bytes 2621440 | tf_op jit(solution)/shard_map/all_to_all | solution.py:195
  82.1 11.4 %copy-start.7 = (bf16[32,40,512]{2,1,0:T(8,128)(2,1)}, bf16[32,40,512]{2,1,0:T(8,128)(2,1)S(1)}, u32[]{:S(2)}) copy-start(bf16[32,40,512]{2,1,0:T(8,128)(2,1)S(1)} %all-to-all-done.4) | copy-start | bytes 3932164
  82.1 35.0 %all-to-all-start.6 = ((bf16[32,40,512]{2,1,0:T(8,128)(2,1)}), bf16[32,40,512]{2,1,0:T(8,128)(2,1)S(1)}, u32[]{:S(2)}, u32[]{:S(2)}) async-start(bf16[32,40,512]{2,1,0:T(8,128)(2,1)} %bitcast.30), calls=%async_computation.6 | async-start | bytes 2621440 | tf_op jit(solution)/shard_map/all_to_all | solution.py:195
  86.6 36.5 %copy-start.10 = (s32[640]{0:T(1024)S(1)}, s32[640]{0:T(1024)}, u32[]{:S(2)}) copy-start(s32[640]{0:T(1024)} %param.6) | copy-start | bytes 7684
  117.1 1.2 copy-start.6
  118.3 35.0 %all-to-all-start.8 = ((bf16[32,40,512]{2,1,0:T(8,128)(2,1)}), bf16[32,40,512]{2,1,0:T(8,128)(2,1)S(1)}, u32[]{:S(2)}, u32[]{:S(2)}) async-start(bf16[32,40,512]{2,1,0:T(8,128)(2,1)} %bitcast.27), calls=%async_computation.8 | async-start | bytes 2621440 | tf_op jit(solution)/shard_map/all_to_all | solution.py:195
  153.3 109.0 %copy-start.5 = (bf16[32,40,512]{2,1,0:T(8,128)(2,1)}, bf16[32,40,512]{2,1,0:T(8,128)(2,1)S(1)}, u32[]{:S(2)}) copy-start(bf16[32,40,512]{2,1,0:T(8,128)(2,1)S(1)} %all-to-all-done.8) | copy-start | bytes 3932164
  153.3 121.6 %all-to-all-start = ((bf16[32,40,512]{2,1,0:T(8,128)(2,1)}), bf16[32,40,512]{2,1,0:T(8,128)(2,1)S(1)}, u32[]{:S(2)}, u32[]{:S(2)}) async-start(bf16[32,40,512]{2,1,0:T(8,128)(2,1)} %bitcast.28), calls=%async_computation | async-start | bytes 2621440 | tf_op jit(solution)/shard_map/all_to_all | solution.py:195
  274.9 18.4 %copy-start.9 = (bf16[32,40,512]{2,1,0:T(8,128)(2,1)}, bf16[32,40,512]{2,1,0:T(8,128)(2,1)S(1)}, u32[]{:S(2)}) copy-start(bf16[32,40,512]{2,1,0:T(8,128)(2,1)S(1)} %all-to-all-done) | copy-start | bytes 3932164
  274.9 36.2 %all-to-all-start.3 = ((bf16[32,40,512]{2,1,0:T(8,128)(2,1)}), bf16[32,40,512]{2,1,0:T(8,128)(2,1)S(1)}, u32[]{:S(2)}, u32[]{:S(2)}) async-start(bf16[32,40,512]{2,1,0:T(8,128)(2,1)} %bitcast.44), calls=%async_computation.3 | async-start | bytes 2621440 | tf_op jit(solution)/shard_map/all_to_all | solution.py:195
  311.1 17.2 %copy-start = (bf16[32,40,512]{2,1,0:T(8,128)(2,1)}, bf16[32,40,512]{2,1,0:T(8,128)(2,1)S(1)}, u32[]{:S(2)}) copy-start(bf16[32,40,512]{2,1,0:T(8,128)(2,1)S(1)} %all-to-all-done.3) | copy-start | bytes 3932164
  311.1 35.0 %all-to-all-start.5 = ((bf16[32,40,512]{2,1,0:T(8,128)(2,1)}), bf16[32,40,512]{2,1,0:T(8,128)(2,1)S(1)}, u32[]{:S(2)}, u32[]{:S(2)}) async-start(bf16[32,40,512]{2,1,0:T(8,128)(2,1)} %bitcast.45), calls=%async_computation.5 | async-start | bytes 2621440 | tf_op jit(solution)/shard_map/all_to_all | solution.py:195
  346.1 17.4 %copy-start.1 = (bf16[32,40,512]{2,1,0:T(8,128)(2,1)}, bf16[32,40,512]{2,1,0:T(8,128)(2,1)S(1)}, u32[]{:S(2)}) copy-start(bf16[32,40,512]{2,1,0:T(8,128)(2,1)S(1)} %all-to-all-done.5) | copy-start | bytes 3932164
  346.1 35.0 %all-to-all-start.7 = ((bf16[32,40,512]{2,1,0:T(8,128)(2,1)}), bf16[32,40,512]{2,1,0:T(8,128)(2,1)S(1)}, u32[]{:S(2)}, u32[]{:S(2)}) async-start(bf16[32,40,512]{2,1,0:T(8,128)(2,1)} %bitcast.46), calls=%async_computation.7 | async-start | bytes 2621440 | tf_op jit(solution)/shard_map/all_to_all | solution.py:195
  381.2 17.2 %copy-start.2 = (bf16[32,40,512]{2,1,0:T(8,128)(2,1)}, bf16[32,40,512]{2,1,0:T(8,128)(2,1)S(1)}, u32[]{:S(2)}) copy-start(bf16[32,40,512]{2,1,0:T(8,128)(2,1)S(1)} %all-to-all-done.7) | copy-start | bytes 3932164
  381.2 35.0 %all-to-all-start.9 = ((bf16[32,40,512]{2,1,0:T(8,128)(2,1)}), bf16[32,40,512]{2,1,0:T(8,128)(2,1)S(1)}, u32[]{:S(2)}, u32[]{:S(2)}) async-start(bf16[32,40,512]{2,1,0:T(8,128)(2,1)} %bitcast.43), calls=%async_computation.9 | async-start | bytes 2621440 | tf_op jit(solution)/shard_map/all_to_all | solution.py:195
  416.2 15.1 %copy-start.3 = (bf16[32,40,512]{2,1,0:T(8,128)(2,1)}, bf16[32,40,512]{2,1,0:T(8,128)(2,1)S(1)}, u32[]{:S(2)}) copy-start(bf16[32,40,512]{2,1,0:T(8,128)(2,1)S(1)} %all-to-all-done.9) | copy-start | bytes 3932164
  416.2 35.0 %all-to-all-start.1 = ((bf16[32,40,512]{2,1,0:T(8,128)(2,1)}), bf16[32,40,512]{2,1,0:T(8,128)(2,1)S(1)}, u32[]{:S(2)}, u32[]{:S(2)}) async-start(bf16[32,40,512]{2,1,0:T(8,128)(2,1)} %bitcast.42), calls=%async_computation.1 | async-start | bytes 2621440 | tf_op jit(solution)/shard_map/all_to_all | solution.py:195
  451.3 1.1 copy-start.4
